TPU v7x, 128 devices: a whole 4x4x4 slice. The times are simulated.
128 devices in a mesh: clus: 16 (over x, y), col: 8 (over z, core).
Axes of the slice: x: 4, y: 4, z: 4, core: 2. Of those that a mesh axis runs over, the one named last changes fastest.
Arguments:
- density: bfloat16 [8192, 8192], P('clus', 'col'), may hold values from -6 to 6
- dens_pattern: int32 [32, 32], P('clus', 'col'), may hold values 0 or 1
- margin_window: bfloat16 [8192, 4096], P('col', 'clus'), may hold values from -0.0625 to 0.0625
- ovl_pattern: int32 [32, 16], P('col', 'clus'), may hold values 0 or 1
- keep_mask: int32 [16, 16], P('clus', 'col'), may hold values 0 or 1
- basis_values: bfloat16 [32, 256, 4096], P('col'), may hold values from -0.375 to 0.375
- rest_density: float32 [256, 256, 256], P('clus', 'col'), may hold values from -0.6 to 0.6
- slab_owner: int32 [32], replicated, may hold values from 0 to 15
- cell_lengths: float32 [3], replicated, may hold values from 200 to 260
Outputs:
- potential: float32 [256, 256, 256], P('clus', 'col')
- hartree: bfloat16 [8192, 8192], P('clus', 'col')
- product: bfloat16 [4096, 4096], P('clus', 'col')
All inputs are finite; a program needn't handle non-finite values. No bound on the sum of `dens_pattern` or of `ovl_pattern` or of `keep_mask` on one device may be relied on, other than what follows from the above.
Results may differ from a plain program's by a relative error of at most 0.0049.
Values may be sent and summed in bfloat16 or wider, within the bound.
A program may use at most 128 MiB of HBM per device.

v0:
```python
import functools
import math

import jax
import jax.numpy as jnp
import ml_dtypes
import numpy as np
from jax import lax
from jax.experimental import pallas as pl
from jax.experimental.pallas import tpu as pltpu
from jax.sharding import PartitionSpec as P

B = 256
G = 256
QZ = 128
NX, NY, NZ = 4, 4, 4
ND = 128
CH = 512
four_pi = 4.0 * math.pi
f32 = jnp.float32
bf16 = jnp.bfloat16
MESH = pl.DeviceIdType.MESH
NT = (((1,), (1,)), ((), ()))
TN = (((0,), (0,)), ((), ()))
NN = (((1,), (0,)), ((), ()))


def split_np(a):
    hi = a.astype(np.float32).astype(ml_dtypes.bfloat16)
    lo = (a - hi.astype(np.float64)).astype(np.float32).astype(ml_dtypes.bfloat16)
    return [hi, lo]


def x_of_row(row):
    return (row % 64) // 4 * 16 + row % 4 * 4 + row // 64


@functools.lru_cache(maxsize=1)
def tables():
    n = np.arange(G)
    ang = 2.0 * np.pi * (n[:, None] * n[None, :] % G) / G
    cos, sin = np.cos(ang), np.sin(ang)
    half = cos[:128], sin[:128]
    tz = np.concatenate([half[0], -half[1]], 0)
    tz[128] = cos[128]
    tzi = np.concatenate([2.0 * half[0], -2.0 * half[1]], 0)
    tzi[0] = 1.0
    tzi[128] = cos[128]
    tzi = tzi / float(G) ** 3
    perm = x_of_row(n)
    wx = np.concatenate([cos[:, perm], sin[:, perm]], 0)
    wi = np.concatenate([cos[perm], sin[perm]], 0)
    tp = np.concatenate([tzi[:128, 64:192], tzi[128:, 64:192]], 1)
    row = np.arange(1024)
    c, l, il, j = row // 64, row // 8 % 8, row // 4 % 2, row % 4
    y = l * 32 + (2 * c + il) // 16 * 4 + j
    sel_y = (y[:, None] == n[None, :]).astype(np.float64)
    sel_y = [sel_y.astype(np.float32).astype(ml_dtypes.bfloat16)]
    t1 = np.concatenate(split_np(tz) + split_np(tzi) + split_np(wx) + split_np(wi) + split_np(tp) + sel_y, 0)
    ty = np.concatenate(split_np(np.concatenate([cos, sin], 1)), 0)
    ri, il, y = row // 512, row // 256 % 2, row % 256
    lane = ri * 64 + il * 32 + y // 32 * 4 + y % 4
    sel_c = (lane[:, None] == np.arange(128)[None, :]) & (y % 32 < 8)[:, None]
    sel_c = sel_c.astype(np.float32).astype(ml_dtypes.bfloat16)
    tzp = np.zeros((ND, 8, 128), np.float32)
    tzp[:, 0] = tz[:128, 64:192]
    tzp[:, 1] = tz[128:, 64:192]
    return t1, ty, sel_c, tzp


ROWS = {}
at = 0
for name, rows in (
    ("tz", 256), ("tzi", 256), ("wx", 512), ("wi", 512), ("tp", 128)
):
    ROWS[name] = (at, rows)
    at += 2 * rows
ROWS["sel_y"] = (at, 1024)
T1_ROWS = at + 1024


def split2(a):
    hi = a.astype(bf16)
    lo = (a - hi.astype(f32)).astype(bf16)
    return hi, lo


def dot(a, b, dims=NN):
    return lax.dot_general(a, b, dims, preferred_element_type=f32)


def dot3(a, b, dims=NN):
    return dot(a[0], b[0], dims) + (dot(a[0], b[1], dims) + dot(a[1], b[0], dims))


def kernel(
    pat_ref, len_ref, dens_ref, phi_ref, rest_ref, xcell_ref, own_ref,
    t1_hbm, ty_hbm, selc_hbm, tzp_hbm,
    pot_ref, har_ref,
    phi, rblk, relay, masked, wt, t1, ty, selc, tzp,
    s1, r1, s2, r2, s3, r3, rp, rq, rho, rg, xa, ga, gb, big,
    lsem, tsem, rsem, ssem, a_s, a_r, q_s, q_r, g_s, g_r, p_s, p_r, b_s, b_r,
):
    c = lax.axis_index("clus")
    k = lax.axis_index("col")
    me = c * 8 + k
    x, y = c // 4, c % 4
    z, h = k // 2, k % 2
    zp, zm, z2 = (z + 1) % 4, (z + 3) % 4, (z + 2) % 4
    root = h == y // 2
    hub = x == z
    far = jnp.logical_not(hub)
    twin = (c, z * 2 + 1 - h)

    def part(name, lo):
        first, rows = ROWS[name]
        return t1[pl.ds(first + lo * rows, rows), :]

    def table(name):
        return part(name, 0), part(name, 1)

    def local(src, dst, sem):
        return pltpu.make_async_copy(src, dst, sem)

    def remote(src, dst, send, recv, to):
        return pltpu.make_async_remote_copy(
            src_ref=src, dst_ref=dst, send_sem=send, recv_sem=recv, device_id=to, device_id_type=MESH
        )

    def others(fn):
        def body(i, carry):
            p = lax.rem(me + i, ND)
            fn(p, (p // 8, p % 8))
            return carry

        lax.fori_loop(1, ND, body, 0)

    bar = pltpu.get_barrier_semaphore()
    others(lambda p, to: pl.semaphore_signal(bar, inc=1, device_id=to, device_id_type=MESH))
    loads = [
        local(t1_hbm, t1, lsem.at[0]),
        local(phi_ref, phi, lsem.at[1]),
        local(ty_hbm, ty, lsem.at[2]),
        local(selc_hbm, selc, lsem.at[3]),
        local(tzp_hbm.at[me], tzp, lsem.at[4]),
    ]
    for copy in loads:
        copy.start()
    for i in range(2):
        for j in range(4):
            keep = pat_ref[i, j].astype(f32).astype(bf16)
            at_rows, at_cols = pl.ds(i * B, B), pl.ds(j * B, B)
            masked[at_rows, at_cols] = dens_ref[at_rows, at_cols] * keep
    loads[0].wait()
    lines = dot3(table("tz"), split2(rest_ref[...]), NT)
    for i in range(2):
        for j in range(4):
            s1[:, i * 4 + j, :] = lines[i * 128 : (i + 1) * 128, j * 128 : (j + 1) * 128]
    loads[1].wait()
    pl.semaphore_wait(bar, ND - 1)

    first = 2 * (y % 2)

    def own_part(l):
        return phi.at[pl.ds(first, 2), :, pl.ds(pl.multiple_of(l * CH, CH), CH)]

    to_send = []

    def send(when, src, dst, recv, to):
        index = len(to_send)
        copy = remote(src, dst, ssem.at[index], recv, to)
        to_send.append((when, copy))
        pl.when(when)(copy.start)

    for up, half in ((True, 0), (False, 1), (True, 1), (False, 0)):
        slot = 0 if up else 1
        send(
            root, own_part(2 * x + half), relay.at[slot], tsem.at[slot],
            (c, (zp if up else zm) * 2 + half),
        )
    hub_root = jnp.logical_and(hub, root)
    for l in range(8):
        send(hub_root, own_part(l), rblk.at[l], rsem.at[l], twin)

        @pl.when(hub_root)
        def _():
            local(own_part(l), rblk.at[l], rsem.at[l]).start()

    others(lambda p, to: remote(s1.at[p], r1.at[c, k], a_s, a_r, to).start())
    local(s1.at[me], r1.at[c, k], a_r).start()

    mine = 2 * x + h
    for slot, plane in ((0, zm), (1, zp), (2, z2)):
        local(relay.at[slot], relay.at[slot], tsem.at[slot]).wait()
        if slot == 0:
            send(h == 0, relay.at[0], relay.at[2], tsem.at[2], (c, zp * 2))
        if slot == 1:
            send(h == 1, relay.at[1], relay.at[2], tsem.at[2], (c, zm * 2 + 1))
        here = plane == x
        send(here, relay.at[slot], rblk.at[mine], rsem.at[mine], twin)
        send(jnp.logical_not(here), relay.at[slot], rblk.at[mine], rsem.at[mine], (plane * 4 + y, k))

        @pl.when(here)
        def _():
            local(relay.at[slot], rblk.at[mine], rsem.at[mine]).start()

    row_id = lax.broadcasted_iota(jnp.int32, (G, G), 0)
    col_id = lax.broadcasted_iota(jnp.int32, (G, G), 1)

    def wave(freq, axis):
        signed = jnp.where(freq < G // 2, freq, freq - G).astype(f32)
        scaled = signed * (2.0 * math.pi) / jnp.full(freq.shape, len_ref[axis], f32)
        return scaled * scaled

    flat = wave(row_id, 0) + wave(col_id, 1)
    for out, kz in ((ga, me), (gb, jnp.where(me == 0, 128, me))):
        kz = jnp.full((G, G), kz, jnp.int32)
        anchor = (row_id == 0) & (col_id == 0) & (kz == 0)
        out[...] = jnp.where(anchor, 0.0, four_pi / jnp.where(anchor, 1.0, flat + wave(kz, 2)))

    fwd = 25

    def step(t, carry):
        own = (t == 0) | ((t % 2 == 1) & (t < 7))
        dx = jnp.where(own, (t + 1) // 2, jnp.where(t == 7, 3, t // 2 - 1))
        l = 2 * ((x + dx) % 4) + jnp.where(own, h, 1 - h)
        local(rblk.at[l], rblk.at[l], rsem.at[l]).wait()

        @pl.when(own & (dx > 0) & far)
        def _():
            remote(rblk.at[l], rblk.at[l], ssem.at[fwd + dx], rsem.at[l], twin).start()

        cells = pl.ds(pl.multiple_of(l * CH, CH), CH)
        values = phi[:, :, cells].reshape(4 * B, CH)
        for i in range(2):
            lifted = dot(masked[i * B : (i + 1) * B, :], values)
            summed = jnp.sum(rblk[l, i].astype(f32) * lifted, axis=0, keepdims=True)
            for j in range(4):
                rp[l, pl.ds(i * 4 + j, 1), :] = summed[:, j * 128 : (j + 1) * 128]
        away = l != k

        @pl.when(away)
        def _():
            remote(rp.at[l], rq.at[k], q_s.at[l], q_r.at[k], (c, l)).start()

        @pl.when(jnp.logical_not(away))
        def _():
            local(rp.at[l], rq.at[k], q_r.at[k]).start()

        return carry

    lax.fori_loop(0, 8, step, 0)
    for l in range(8):
        local(rq.at[l], rq.at[l], q_r.at[l]).wait()
    rho[...] = jnp.sum(rq[...], axis=0)

    others(lambda p, to: remote(rho, rg.at[me], g_s, g_r, to).start())
    local(rho, rg.at[me], g_r).start()

    lane = lax.broadcasted_iota(jnp.int32, (1, 1, 128), 2) // 32
    low = lax.broadcasted_iota(jnp.int32, (1, 8, 1), 1) < 4
    local(r1, r1, a_r).wait()
    for kk in range(2):
        got = [r1[:, kk * 4 + k4] for k4 in range(4)]
        for p4 in range(4):
            tile = got[p4]
            for k4 in range(4):
                if k4 != p4:
                    turned = pltpu.roll(got[k4], (k4 - p4) % 4 * 32, 2)
                    tile = jnp.where(lane == k4, turned, tile)
            pairs = tile.reshape(8, 2, 8, 128)
            even, odd = pairs[:, 0], pairs[:, 1]
            at_rows, at_cols = pl.ds(p4 * 64, 64), pl.ds(kk * 128, 128)
            xa[at_rows, at_cols] = jnp.where(low, even, pltpu.roll(odd, 4, 1)).reshape(64, 128)
            xa[pl.ds(256 + p4 * 64, 64), at_cols] = jnp.where(low, pltpu.roll(even, 4, 1), odd).reshape(64, 128)

    for copy in loads[2:]:
        copy.wait()
    row_x = x_of_row(lax.broadcasted_iota(jnp.int32, (G, 1), 0))
    sits = row_x == xcell_ref[...]
    local(rg, rg, g_r).wait()
    coef = lax.dot_general(
        tzp[...], rg[...].reshape(8 * ND, QZ), NT,
        precision=lax.Precision.HIGHEST, preferred_element_type=f32,
    )
    sel_first, sel_rows = ROWS["sel_y"]
    sel_y = t1[pl.ds(sel_first, sel_rows), :]
    for i in range(2):
        add = None
        for piece in split2(coef[i : i + 1, :]):
            placed = jnp.where(sits, piece.astype(f32), 0.0).astype(bf16)
            term = dot(placed, sel_y)
            add = term if add is None else add + term
        xa[pl.ds(i * G, G), :] = xa[pl.ds(i * G, G), :] + add

    ty_pair = ty[0:G, :], ty[G : 2 * G, :]
    big[...] = dot3(split2(xa[...]), ty_pair)
    wx = table("wx")
    fields = []
    for i in range(2):
        quad = dot3(wx, split2(big[pl.ds(i * G, G), :]))
        fields.append((quad[:G, :G] - quad[G:, G:], -(quad[G:, :G] + quad[:G, G:])))
    (a_re, a_im), (b_re, b_im) = fields
    xa[0:G, :] = ga[...] * a_re - gb[...] * b_im
    xa[G : 2 * G, :] = ga[...] * a_im + gb[...] * b_re
    back = dot3(split2(xa[...]), ty_pair)
    big[0:G, 0:G] = back[:G, :G] - back[G:, G:]
    big[0:G, G : 2 * G] = back[:G, G:] + back[G:, :G]
    quad = dot3(table("wi"), split2(big[0:G, :]))
    xa[0:G, :] = quad[:G, :G] - quad[G:, G:]
    xa[G : 2 * G, :] = quad[:G, G:] + quad[G:, :G]

    order = lax.broadcasted_iota(jnp.int32, (32, G), 0)
    block = order % 16 * 2 + order // 16
    row_of = x_of_row(lax.broadcasted_iota(jnp.int32, (32, G), 1))
    pick = (row_of == own_ref[...] * 16 + block % 16).astype(f32).astype(bf16)
    line = lax.broadcasted_iota(jnp.int32, (32, G), 1)
    valid = line % 32 // 4 == block // 16
    rows = []
    for i in range(2):
        hi, lo = split2(xa[pl.ds(i * G, G), :])
        here = jnp.where(valid, dot(pick, hi) + dot(pick, lo), 0.0)
        rows += [here[0:16], here[16:32]]
    hi, lo = split2(jnp.concatenate(rows, axis=1))
    packed = dot(hi, selc[...]) + dot(lo, selc[...])
    for i in range(16):
        s3[i] = packed[i : i + 1, :]
    others(lambda p, to: remote(s3.at[p // 8], r3.at[me], p_s, p_r, to).start())
    local(s3.at[c], r3.at[me], p_r).start()

    for kk in range(2):
        tiles = []
        at_cols = pl.ds(kk * 128, 128)
        for p4 in range(4):
            re = xa[pl.ds(p4 * 64, 64), at_cols].reshape(8, 8, 128)
            im = xa[pl.ds(256 + p4 * 64, 64), at_cols].reshape(8, 8, 128)
            even = jnp.where(low, re, pltpu.roll(im, 4, 1))
            odd = jnp.where(low, pltpu.roll(re, 4, 1), im)
            tiles.append(jnp.stack([even, odd], axis=1).reshape(16, 8, 128))
        for k4 in range(4):
            tile = tiles[k4]
            for p4 in range(4):
                if p4 != k4:
                    tile = jnp.where(lane == p4, pltpu.roll(tiles[p4], (p4 - k4) % 4 * 32, 2), tile)
            s2[:, kk * 4 + k4] = tile
    others(lambda p, to: remote(s2.at[p // 8, p % 8], r2.at[me], b_s, b_r, to).start())
    local(s2.at[c, k], r2.at[me], b_r).start()

    local(r3, r3, p_r).wait()
    arrived = split2(r3[...].reshape(ND, 128))
    both = dot3(arrived, table("tp"), TN)
    rho_pot = both[:64, :128] + both[64:, 128:]
    for i in range(2):
        for l in range(8):
            for j in range(4):
                at_row = i * 32 + l * 4 + j
                scaled = rblk[l, i, :, pl.ds(j * 128, 128)].astype(f32) * rho_pot[at_row : at_row + 1, :]
                wt[pl.ds(i * B, B), pl.ds(l * CH + j * 128, 128)] = scaled.astype(bf16)
    for j in range(4):
        for i in range(2):
            block_sum = dot(wt[pl.ds(i * B, B), :], phi[j], NT)
            har_ref[pl.ds(i * B, B), pl.ds(j * B, B)] = (block_sum * pat_ref[i, j].astype(f32)).astype(bf16)

    local(r2, r2, b_r).wait()
    tzi = table("tzi")
    for j in range(4):
        got = jnp.concatenate([r2[:, j, :], r2[:, 4 + j, :]], axis=0)
        pot_ref[pl.ds(j * 128, 128), :] = dot3(split2(got), tzi, TN)

    for when, copy in to_send:
        pl.when(when)(copy.wait_send)
    for dx in range(1, 4):
        l = 2 * ((x + dx) % 4) + h

        @pl.when(far)
        def _():
            remote(rblk.at[l], rblk.at[l], ssem.at[fwd + dx], rsem.at[l], twin).wait_send()

    for l in range(8):

        @pl.when(l != k)
        def _():
            remote(rp.at[l], rq.at[k], q_s.at[l], q_r.at[k], (c, l)).wait_send()

    most = pl.ds(0, ND - 1)
    for src, sem in ((s1, a_s), (rg, g_s), (r3, p_s), (r2, b_s)):
        local(src.at[most], src.at[most], sem).wait()


def main_call(density, pattern, basis, rest, slab_owner, lengths):
    t1, ty, selc, tzp = tables()
    blocks = jnp.arange(32, dtype=jnp.int32)
    x_cells = slab_owner * 16 + blocks % 16
    xcell = jnp.broadcast_to(x_cells.reshape(16, 1, 2, 1), (16, 8, 2, 4)).reshape(1, 1024)
    order = slab_owner.reshape(16, 2).T.reshape(32, 1)
    vmem = pl.BlockSpec(memory_space=pltpu.VMEM)
    smem = pl.BlockSpec(memory_space=pltpu.SMEM)
    hbm = pl.BlockSpec(memory_space=pl.ANY)
    V = pltpu.VMEM
    D = pltpu.SemaphoreType.DMA
    return pl.pallas_call(
        kernel,
        out_shape=(
            jax.ShapeDtypeStruct((512, G), f32),
            jax.ShapeDtypeStruct((512, 1024), bf16),
        ),
        in_specs=[smem, smem, vmem, hbm, vmem, vmem, vmem, hbm, hbm, hbm, hbm],
        out_specs=(vmem, vmem),
        scratch_shapes=[
            V((4, B, 4096), bf16),
            V((8, 2, B, CH), bf16),
            V((3, 2, B, CH), bf16),
            V((512, 1024), bf16),
            V((512, 4096), bf16),
            V((T1_ROWS, G), bf16),
            V((2 * G, 2 * G), bf16),
            V((1024, 128), bf16),
            V((8, 128), f32),
            V((ND, 8, 128), f32),
            V((16, 8, 8, 128), f32),
            V((16, 8, 8, 128), f32),
            V((ND, 8, 128), f32),
            V((16, 1, 128), f32),
            V((ND, 1, 128), f32),
            V((8, 8, 128), f32),
            V((8, 8, 128), f32),
            V((8, 128), f32),
            V((ND, 8, 128), f32),
            V((2 * G, G), f32),
            V((G, G), f32),
            V((G, G), f32),
            V((2 * G, 2 * G), f32),
            D((5,)),
            D((3,)),
            D((8,)),
            D((32,)),
            D(()),
            D(()),
            D((8,)),
            D((8,)),
            D(()),
            D(()),
            D(()),
            D(()),
            D(()),
            D(()),
        ],
        compiler_params=pltpu.CompilerParams(
            collective_id=0, has_side_effects=True, vmem_limit_bytes=56 << 20
        ),
        cost_estimate=pl.CostEstimate(flops=12 * 10**9, bytes_accessed=24 << 20, transcendentals=0),
    )(pattern, lengths, density, basis, rest, xcell, order, t1, ty, selc, tzp)


def per_device(
    density, dens_pattern, margin_window, ovl_pattern, keep_mask, basis_values, rest_density,
    slab_owner, cell_lengths,
):
    clus_count = lax.axis_size("clus")
    col_count = lax.axis_size("col")
    ratio_cols = clus_count // col_count
    window_rows = (
        density[:B].reshape(B, 4, B) * dens_pattern[0].astype(bf16)[None, :, None]
    ).reshape(B, 4 * B)
    margin_masked = (
        margin_window.reshape(4, B, B) * ovl_pattern.astype(bf16)[:, :, None]
    ).reshape(4 * B, B)
    partial_sums = jnp.dot(
        window_rows, lax.all_gather(margin_masked, "clus", axis=1, tiled=True), preferred_element_type=f32
    )
    summed = lax.psum_scatter(partial_sums, "col", scatter_dimension=1, tiled=True)
    product = (
        (summed.reshape(B, ratio_cols, B) * keep_mask.astype(f32)[0][None, :, None])
        .reshape(B, ratio_cols * B)
        .astype(bf16)
    )
    potential, hartree = main_call(
        density, dens_pattern, basis_values, rest_density.reshape(512, G), slab_owner, cell_lengths
    )
    return potential.reshape(16, 32, G), hartree, product


def solution(mesh):
    return jax.shard_map(
        per_device,
        mesh=mesh,
        in_specs=(
            P("clus", "col"),
            P("clus", "col"),
            P("col", "clus"),
            P("col", "clus"),
            P("clus", "col"),
            P("col", None, None),
            P("clus", "col", None),
            P(),
            P(),
        ),
        out_specs=(P("clus", "col", None), P("clus", "col"), P("clus", "col")),
        check_vma=False,
    )
```

profile of v0, /device:TPU:1, one launch (start us, length us, event | category | flops | bytes accessed | tf_op | source)
XLA Modules:
  0.0 230.3 jit_solution(10410936633063602656)
XLA Ops:
  7.2 0.0 all-gather.2.cloned.1.call-start
  7.2 0.7 convert_bitcast_fusion.1
  7.9 0.1 broadcast_bitcast_fusion.1
  8.0 2.0 broadcast_multiply_fusion
  10.0 0.0 all-gather.2.cloned.1.call-update
  10.0 0.0 reduce-scatter.2.cloned.1.call-start
  10.1 0.7 convert.3
  10.8 0.1 broadcast_bitcast_fusion.2
  10.8 80.4 %all-gather.2.cloned.1.call-done = bf16[1024,4096]{1,0:T(8,128)(2,1)} async-done(((bf16[1024,256]{1,0:T(8,128)(2,1)}), bf16[1024,4096]{1,0:T(8,128)(2,1)}) %all-gather.2.cloned.1.call-update) | async-done | bytes 8388624 | tf_op jit(solution)/shard_map/all_gather | solution.py:469
  91.3 0.0 copy-start.1
  91.3 0.0 copy-start
  91.3 7.9 %fusion = f32[256,4096]{1,0:T(8,128)} fusion(bf16[1024,4096]{1,0:T(8,128)(2,1)} %all-gather.2.cloned.1.call-done, bf16[512,1024]{1,0:T(8,128)(2,1)} %dens_ref.1, bf16[1024]{0:T(1024)(128)(2,1)S(1)} %bitcast.20), kind=kOutput, calls=%fused_computation.1 | convolution fusion | flops 2147745792 | bytes 13109248 | tf_op jit(solution)/shard_map/dot_general | solution.py:468
  99.2 0.0 reduce-scatter.2.cloned.1.call-update
  99.2 0.0 copy-done.1
  99.2 0.1 broadcast_bitcast_fusion
  99.3 0.0 copy-done
  99.3 0.1 reshape.42
  99.4 0.1 broadcast_in_dim.4
  99.5 0.1 copy.18
  99.6 0.7 reshape.45.own_ref
  100.3 0.1 broadcast_in_dim.10
  100.4 0.8 reshape.41.xcell_ref
  101.2 116.3 %shard_map.148 = (f32[512,256]{1,0:T(8,128)}, bf16[512,1024]{1,0:T(8,128)(2,1)}) custom-call(s32[2,4]{1,0:T(2,128)} %pat_ref.1, f32[3]{0:T(128)} %len_ref.1, bf16[512,1024]{1,0:T(8,128)(2,1)} %dens_ref.1, bf16[4,256,4096]{2,1,0:T(8,128)(2,1)} %phi_ref.1, f32[512,256]{1,0:T(8,128)} %bitcast.24, s32[1,1024]{1,0:T(1,128)} %reshape.41.xcell_ref, ...), custom_call_target="tpu_custom_call" | custom-call | flops 12000000000 | bytes 25165824 | tf_op jit(solution)/shard_map/pallas_call | solution.py:401
  217.5 0.0 reduce-scatter.2.cloned.1.call-done
  217.5 1.8 multiply_convert_fusion
  219.3 1.9 copy.25
  221.2 2.3 copy.26
  (6 shorter events, 0.0 us)
Async XLA Ops:
  7.2 84.1 %all-gather.2.cloned.1.call-start = ((), (), s32[]{:S(2)}) async-start(), calls=%async_computation.1 | async-start | bytes 8912896 | tf_op jit(solution)/shard_map/all_gather | solution.py:469
  10.0 207.5 %reduce-scatter.2.cloned.1.call-start = ((), (), s32[]{:S(2)}) async-start(), calls=%async_computation.2 | async-start | bytes 4718592 | tf_op jit(solution)/shard_map/reduce_scatter | solution.py:471
  91.3 7.9 %copy-start.1 = (s32[1,2]{1,0:T(1,128)S(1)}, s32[1,2]{1,0:T(1,128)}, u32[]{:S(2)}) copy-start(s32[1,2]{1,0:T(1,128)} %param.17) | copy-start | bytes 28
  91.3 8.0 %copy-start = (s32[32]{0:T(128)S(1)}, s32[32]{0:T(128)}, u32[]{:S(2)}) copy-start(s32[32]{0:T(128)} %param.20) | copy-start | bytes 388
Sparse Core Ops, SparseCore 0:
  10.7 80.5 all-gather.1
  99.3 53.0 reduce-scatter.1
where the time goes:
time: 231 us; the launch traced here: 230 us
  Pallas kernels  116 us (50%)
  waiting for transfers between devices  80.5 us (35%)
  between operations  14.1 us (6%)
  matrix products  7.89 us (3%)
  local copies, waits for them, and re-layouts  6.24 us (3%)
  other arithmetic  5.17 us (2%)
    pallas_call x1, Pallas kernels, main_call(): pl.pallas_call(kernel, out_shape=(jax.ShapeDtypeStruct((512, G), f32), ja...  116 us
    all_gather x1, waiting for transfers between devices, per_device(): lax.all_gather(margin_masked, 'clus', axis=1, tiled=True)  80.4 us
    dot_general x1, matrix products, per_device(): jnp.dot(window_rows, lax.all_gather(margin_masked, 'clus', axis=1, tiled=...  7.89 us
  transfers between devices with their start and end apart: 2, of which 1 were waited for; matrix products, arithmetic and copies ran while one was open for 1% of the time, Pallas kernels for 51%

commit v1 on v0

--- a/solution.py
+++ b/solution.py
@@ -94,12 +94,14 @@
 
 
 def kernel(
-    pat_ref, len_ref, dens_ref, phi_ref, rest_ref, xcell_ref, own_ref,
+    pat_ref, len_ref, ovl_ref, keep_ref, margin_ref, dens_ref, phi_ref, rest_ref, xcell_ref, own_ref,
     t1_hbm, ty_hbm, selc_hbm, tzp_hbm,
-    pot_ref, har_ref,
+    pot_ref, har_ref, prod_ref,
     phi, rblk, relay, masked, wt, t1, ty, selc, tzp,
     s1, r1, s2, r2, s3, r3, rp, rq, rho, rg, xa, ga, gb, big,
+    wd, wm, tt, trx, zs, zr, ys, yr,
     lsem, tsem, rsem, ssem, a_s, a_r, q_s, q_r, g_s, g_r, p_s, p_r, b_s, b_r,
+    wd_s, wd_r, wm_s, wm_r, tw_s, tw_r, zs_s, zr_r, ys_s, yr_r,
 ):
     c = lax.axis_index("clus")
     k = lax.axis_index("col")
@@ -151,6 +153,10 @@
             keep = pat_ref[i, j].astype(f32).astype(bf16)
             at_rows, at_cols = pl.ds(i * B, B), pl.ds(j * B, B)
             masked[at_rows, at_cols] = dens_ref[at_rows, at_cols] * keep
+    wd[y] = masked[0:B, :]
+    for j in range(4):
+        at_rows = pl.ds(j * B, B)
+        wm[x, at_rows, :] = margin_ref[at_rows, :] * ovl_ref[j, 0].astype(f32).astype(bf16)
     loads[0].wait()
     lines = dot3(table("tz"), split2(rest_ref[...]), NT)
     for i in range(2):
@@ -158,6 +164,13 @@
             s1[:, i * 4 + j, :] = lines[i * 128 : (i + 1) * 128, j * 128 : (j + 1) * 128]
     loads[1].wait()
     pl.semaphore_wait(bar, ND - 1)
+
+    to_y = [(x * 4 + (y + i) % 4, k) for i in range(1, 4)]
+    to_x = [((x + i) % 4 * 4 + y, k) for i in range(1, 4)]
+    rows_out = [remote(wd.at[y], wd.at[y], wd_s.at[i], wd_r.at[y], to) for i, to in enumerate(to_y)]
+    cols_out = [remote(wm.at[x], wm.at[x], wm_s.at[i], wm_r.at[x], to) for i, to in enumerate(to_x)]
+    for copy in rows_out:
+        copy.start()
 
     first = 2 * (y % 2)
 
@@ -185,6 +198,9 @@
         @pl.when(hub_root)
         def _():
             local(own_part(l), rblk.at[l], rsem.at[l]).start()
+
+    for copy in cols_out:
+        copy.start()
 
     others(lambda p, to: remote(s1.at[p], r1.at[c, k], a_s, a_r, to).start())
     local(s1.at[me], r1.at[c, k], a_r).start()
@@ -250,12 +266,43 @@
         return carry
 
     lax.fori_loop(0, 8, step, 0)
+
+    for i in range(1, 4):
+        ny, nx = (y + i) % 4, (x + i) % 4
+        local(wd.at[ny], wd.at[ny], wd_r.at[ny]).wait()
+        local(wm.at[nx], wm.at[nx], wm_r.at[nx]).wait()
+
+    def tile_step(t, carry):
+        tt[t % 4 // 2, t // 4, t % 2] = dot(wd[t // 4], wm[t % 4])
+        return carry
+
+    lax.fori_loop(0, 16, tile_step, 0)
+    swap = remote(tt.at[1 - h], trx, tw_s, tw_r, twin)
+    swap.start()
     for l in range(8):
         local(rq.at[l], rq.at[l], q_r.at[l]).wait()
     rho[...] = jnp.sum(rq[...], axis=0)
 
     others(lambda p, to: remote(rho, rg.at[me], g_s, g_r, to).start())
     local(rho, rg.at[me], g_r).start()
+
+    swap.wait_recv()
+    side = y // 2
+
+    def to_collect(i):
+        target = 2 * h + i
+        stays = (target == z) & (side == h)
+        return stays, remote(zs.at[i], zr.at[z], zs_s.at[i], zr_r.at[z], (c, target * 2 + side))
+
+    for i in range(2):
+        for j in range(4):
+            zs[i, j] = (tt[h, j, i] + trx[j, i]).astype(bf16)
+        stays, copy = to_collect(i)
+        pl.when(jnp.logical_not(stays))(copy.start)
+
+        @pl.when(stays)
+        def _():
+            local(zs.at[i], zr.at[z], zr_r.at[z]).start()
 
     lane = lax.broadcasted_iota(jnp.int32, (1, 1, 128), 2) // 32
     low = lax.broadcasted_iota(jnp.int32, (1, 8, 1), 1) < 4
@@ -327,6 +374,23 @@
         s3[i] = packed[i : i + 1, :]
     others(lambda p, to: remote(s3.at[p // 8], r3.at[me], p_s, p_r, to).start())
     local(s3.at[c], r3.at[me], p_r).start()
+
+    collects = h == side
+
+    def to_owner(j):
+        ny = (y + j) % 4
+        return remote(ys.at[ny], yr.at[y % 2], ys_s.at[j - 1], yr_r.at[y % 2], (x * 4 + ny, k))
+
+    @pl.when(collects)
+    def _():
+        for i in range(4):
+            local(zr.at[i], zr.at[i], zr_r.at[i]).wait()
+        for j in range(4):
+            total = zr[0, j].astype(f32) + zr[1, j].astype(f32) + (zr[2, j].astype(f32) + zr[3, j].astype(f32))
+            ys[j] = total.astype(bf16)
+        for j in range(1, 4):
+            to_owner(j).start()
+        local(ys.at[y], yr.at[y % 2], yr_r.at[y % 2]).start()
 
     for kk in range(2):
         tiles = []
@@ -367,6 +431,21 @@
         got = jnp.concatenate([r2[:, j, :], r2[:, 4 + j, :]], axis=0)
         pot_ref[pl.ds(j * 128, 128), :] = dot3(split2(got), tzi, TN)
 
+    for i in range(2):
+        local(yr.at[i], yr.at[i], yr_r.at[i]).wait()
+        prod_ref[:, pl.ds(i * B, B)] = yr[i] * keep_ref[0, i].astype(f32).astype(bf16)
+
+    for copy in rows_out + cols_out + [swap]:
+        copy.wait_send()
+    for i in range(2):
+        stays, copy = to_collect(i)
+        pl.when(jnp.logical_not(stays))(copy.wait_send)
+
+    @pl.when(collects)
+    def _():
+        for j in range(1, 4):
+            to_owner(j).wait_send()
+
     for when, copy in to_send:
         pl.when(when)(copy.wait_send)
     for dx in range(1, 4):
@@ -387,7 +466,7 @@
         local(src.at[most], src.at[most], sem).wait()
 
 
-def main_call(density, pattern, basis, rest, slab_owner, lengths):
+def main_call(density, pattern, margin, ovl, keep, basis, rest, slab_owner, lengths):
     t1, ty, selc, tzp = tables()
     blocks = jnp.arange(32, dtype=jnp.int32)
     x_cells = slab_owner * 16 + blocks % 16
@@ -403,9 +482,10 @@
         out_shape=(
             jax.ShapeDtypeStruct((512, G), f32),
             jax.ShapeDtypeStruct((512, 1024), bf16),
+            jax.ShapeDtypeStruct((B, 2 * B), bf16),
         ),
-        in_specs=[smem, smem, vmem, hbm, vmem, vmem, vmem, hbm, hbm, hbm, hbm],
-        out_specs=(vmem, vmem),
+        in_specs=[smem] * 4 + [vmem, vmem, hbm, vmem, vmem, vmem, hbm, hbm, hbm, hbm],
+        out_specs=(vmem, vmem, vmem),
         scratch_shapes=[
             V((4, B, 4096), bf16),
             V((8, 2, B, CH), bf16),
@@ -430,6 +510,14 @@
             V((G, G), f32),
             V((G, G), f32),
             V((2 * G, 2 * G), f32),
+            V((4, B, 1024), bf16),
+            V((4, 1024, B), bf16),
+            V((2, 4, 2, B, B), f32),
+            V((4, 2, B, B), f32),
+            V((2, 4, B, B), bf16),
+            V((4, 4, B, B), bf16),
+            V((4, B, B), bf16),
+            V((2, B, B), bf16),
             D((5,)),
             D((3,)),
             D((8,)),
@@ -444,38 +532,31 @@
             D(()),
             D(()),
             D(()),
+            D((3,)),
+            D((4,)),
+            D((3,)),
+            D((4,)),
+            D(()),
+            D(()),
+            D((2,)),
+            D((4,)),
+            D((3,)),
+            D((2,)),
         ],
         compiler_params=pltpu.CompilerParams(
-            collective_id=0, has_side_effects=True, vmem_limit_bytes=56 << 20
+            collective_id=0, has_side_effects=True, vmem_limit_bytes=58 << 20
         ),
         cost_estimate=pl.CostEstimate(flops=12 * 10**9, bytes_accessed=24 << 20, transcendentals=0),
-    )(pattern, lengths, density, basis, rest, xcell, order, t1, ty, selc, tzp)
+    )(pattern, lengths, ovl, keep, margin, density, basis, rest, xcell, order, t1, ty, selc, tzp)
 
 
 def per_device(
     density, dens_pattern, margin_window, ovl_pattern, keep_mask, basis_values, rest_density,
     slab_owner, cell_lengths,
 ):
-    clus_count = lax.axis_size("clus")
-    col_count = lax.axis_size("col")
-    ratio_cols = clus_count // col_count
-    window_rows = (
-        density[:B].reshape(B, 4, B) * dens_pattern[0].astype(bf16)[None, :, None]
-    ).reshape(B, 4 * B)
-    margin_masked = (
-        margin_window.reshape(4, B, B) * ovl_pattern.astype(bf16)[:, :, None]
-    ).reshape(4 * B, B)
-    partial_sums = jnp.dot(
-        window_rows, lax.all_gather(margin_masked, "clus", axis=1, tiled=True), preferred_element_type=f32
-    )
-    summed = lax.psum_scatter(partial_sums, "col", scatter_dimension=1, tiled=True)
-    product = (
-        (summed.reshape(B, ratio_cols, B) * keep_mask.astype(f32)[0][None, :, None])
-        .reshape(B, ratio_cols * B)
-        .astype(bf16)
-    )
-    potential, hartree = main_call(
-        density, dens_pattern, basis_values, rest_density.reshape(512, G), slab_owner, cell_lengths
+    potential, hartree, product = main_call(
+        density, dens_pattern, margin_window, ovl_pattern, keep_mask, basis_values,
+        rest_density.reshape(512, G), slab_owner, cell_lengths,
     )
     return potential.reshape(16, 32, G), hartree, product
 

time: 231 us -> 123 us (0.53)
  waiting for transfers between devices: 80.5 us -> 0 us
  between operations: 14.1 us -> 0.65 us
  matrix products: 7.89 us -> 0 us
  Pallas kernels: 116 us -> 111 us
  other arithmetic: 5.17 us -> 0.66 us
  local copies, waits for them, and re-layouts: 6.24 us -> 9.63 us
    all_gather x1 -> x0, waiting for transfers between devices: 80.4 us -> none  [per_device(): lax.all_gather(margin_masked, 'clus', axis=1, tiled=True)]
    dot_general x1 -> x0, matrix products: 7.89 us -> none  [per_device(): jnp.dot(window_rows, lax.all_gather(margin_masked, 'clus', axis=1, tiled=...]
    pallas_call x1, Pallas kernels: 116 us -> 111 us  [main_call(): pl.pallas_call(kernel, out_shape=(jax.ShapeDtypeStruct((512, G), f32), ja...]
    unnamed x12 -> x4, local copies, waits for them, and re-layouts: 4.39 us -> 7.12 us
    mul x3 -> x0, other arithmetic: 2.7 us -> none  [the longest x2 2.7 us: per_device(): margin_window.reshape(4, B, B) * ovl_pattern.astype(bf16)[:, :, None]]
  transfers between devices with their start and end apart: 2 -> 0, of which waited for: 1 -> 0; matrix products, arithmetic and copies ran while one was open for 1% -> 0% of each run, Pallas kernels for 51% -> 0%
where the time goes in v1:
time: 123 us; the launch traced here: 122 us
  Pallas kernels  111 us (90%)
  local copies, waits for them, and re-layouts  9.63 us (8%)
    pallas_call x1, Pallas kernels, main_call(): pl.pallas_call(kernel, out_shape=(jax.ShapeDtypeStruct((512, G), f32), ja...  111 us
    unnamed x4, local copies, waits for them, and re-layouts  7.12 us

profile of v1, /device:TPU:1, one launch (start us, length us, event | category | flops | bytes accessed | tf_op | source)
XLA Modules:
  0.0 122.4 jit_solution(15104179715826928552)
XLA Ops:
  0.6 0.7 fusion
  1.3 1.3 %copy.20.ovl_ref = s32[4,1]{1,0:T(4,128)} copy(s32[4,1]{0,1:T(1,128)} %param.16) | data formatting | bytes 32 | tf_op args[3]
  2.6 0.1 broadcast_in_dim.7
  2.7 0.7 reshape.25
  3.4 0.1 copy.19
  3.5 0.7 reshape.28.own_ref
  4.2 0.1 broadcast_in_dim.8
  4.3 0.8 reshape.24.xcell_ref
  5.1 111.5 %shard_map.148 = (f32[512,256]{1,0:T(8,128)}, bf16[512,1024]{1,0:T(8,128)(2,1)}, bf16[256,512]{1,0:T(8,128)(2,1)}) custom-call(s32[2,4]{1,0:T(2,128)} %pat_ref.1, f32[3]{0:T(128)} %len_ref.1, s32[4,1]{1,0:T(4,128)} %copy.20.ovl_ref, s32[1,2]{1,0:T(1,128)} %keep_ref.1, bf16[1024,256]{1,0:T(8,128)(2,1)} %margin_ref.1, bf16[512,1024]{1,0:T(8,128)(2,1)} %dens_ref.1, ...), custom_call_target="tpu_custom_call" | custom-call | flops 12000000000 | bytes 25165824 | tf_op jit(solution)/shard_map/pallas_call | solution.py:480
  116.6 1.9 %copy.25 = f32[16,32,256]{2,1,0:T(8,128)} copy(f32[16,32,256]{2,1,0:T(8,128)} %bitcast.3) | data formatting | bytes 1048576
  118.5 2.3 %copy.26 = bf16[512,1024]{1,0:T(8,128)(2,1)} copy(bf16[512,1024]{1,0:T(8,128)(2,1)} %get-tuple-element.13) | data formatting | bytes 2097152
  120.7 1.7 %copy.27 = bf16[256,512]{1,0:T(8,128)(2,1)} copy(bf16[256,512]{1,0:T(8,128)(2,1)} %get-tuple-element.14) | data formatting | bytes 524288

commit v2 on v1

v2 whole, which is shorter than its diff:
```python
import functools
import math

import jax
import jax.numpy as jnp
import ml_dtypes
import numpy as np
from jax import lax
from jax.experimental import pallas as pl
from jax.experimental.pallas import tpu as pltpu
from jax.sharding import PartitionSpec as P

B = 256
G = 256
QZ = 128
NX, NY, NZ = 4, 4, 4
ND = 128
CH = 128
NCH = 32
SHARE = (5, 5, 1, 5)
FIRST = (0, 5, 10, 11)
MOST = 5
four_pi = 4.0 * math.pi
f32 = jnp.float32
bf16 = jnp.bfloat16
MESH = pl.DeviceIdType.MESH
NT = (((1,), (1,)), ((), ()))
TN = (((0,), (0,)), ((), ()))
NN = (((1,), (0,)), ((), ()))


def split_np(a):
    hi = a.astype(np.float32).astype(ml_dtypes.bfloat16)
    lo = (a - hi.astype(np.float64)).astype(np.float32).astype(ml_dtypes.bfloat16)
    return [hi, lo]


def x_of_row(row):
    return (row % 64) // 4 * 16 + row % 4 * 4 + row // 64


@functools.lru_cache(maxsize=1)
def tables():
    n = np.arange(G)
    ang = 2.0 * np.pi * (n[:, None] * n[None, :] % G) / G
    cos, sin = np.cos(ang), np.sin(ang)
    half = cos[:128], sin[:128]
    tz = np.concatenate([half[0], -half[1]], 0)
    tz[128] = cos[128]
    tzi = np.concatenate([2.0 * half[0], -2.0 * half[1]], 0)
    tzi[0] = 1.0
    tzi[128] = cos[128]
    tzi = tzi / float(G) ** 3
    perm = x_of_row(n)
    wx = np.concatenate([cos[:, perm], sin[:, perm]], 0)
    wi = np.concatenate([cos[perm], sin[perm]], 0)
    tq = np.concatenate([tz[:128, 64:192], tz[128:, 64:192]], 1)
    kc = np.arange(ND) % 16 * 8 + np.arange(ND) // 16
    tzi = np.concatenate([tzi[:128][kc], tzi[128:][kc]], 0)
    tp = np.concatenate([tzi[:128, 64:192], tzi[128:, 64:192]], 1)
    t1 = np.concatenate(sum([split_np(a) for a in (tz, tzi, wx, wi, tp, tq)], []), 0)
    ty = np.concatenate(split_np(np.concatenate([cos, sin], 1)), 0)
    row = np.arange(1024)
    ri, il, y = row // 512, row // 256 % 2, row % 256
    lane = ri * 64 + il * 32 + y // 32 * 4 + y % 4
    sel_c = (lane[:, None] == np.arange(128)[None, :]) & (y % 32 < 8)[:, None]
    sel_c = sel_c.astype(np.float32).astype(ml_dtypes.bfloat16)
    return t1, ty, sel_c


ROWS = {}
at = 0
for name, rows in (
    ("tz", 256), ("tzi", 256), ("wx", 512), ("wi", 512), ("tp", 128), ("tq", 128)
):
    ROWS[name] = (at, rows)
    at += 2 * rows
T1_ROWS = at


def split2(a):
    hi = a.astype(bf16)
    lo = (a - hi.astype(f32)).astype(bf16)
    return hi, lo


def dot(a, b, dims=NN):
    return lax.dot_general(a, b, dims, preferred_element_type=f32)


def dot3(a, b, dims=NN):
    return dot(a[0], b[0], dims) + (dot(a[0], b[1], dims) + dot(a[1], b[0], dims))


def kernel(
    pat_ref, len_ref, ovl_ref, keep_ref, margin_ref, own_ref, dens_ref, phi_ref, rest_ref,
    t1_hbm, ty_hbm, selc_hbm,
    pot_out, har_out, prod_out,
    pot_ref, har_ref, prod_ref,
    phi, rblk, relay, masked, wt, t1, ty, selc,
    s1, x1, r1, s2, x2, r2, s3, x3, r3, v1, xv, rv, rp, rq, pad, xa, ga, gb, big,
    wd, wm, tt, trx, zs, zr, ys, yr,
    lsem, tsem, rsem, ssem, fsem, q_s, q_r,
    a1_s, a1_r, a2_s, a2_r, g1_s, g1_r, g2_s, g2_r, p1_s, p1_r, p2_s, p2_r, b1_s, b1_r, b2_s, b2_r,
    wd_s, wd_r, wm_s, wm_r, tw_s, tw_r, zs_s, zr_r, ys_s, yr_r, osem,
):
    c = lax.axis_index("clus")
    k = lax.axis_index("col")
    me = c * 8 + k
    x, y = c // 4, c % 4
    z, h = k // 2, k % 2
    zp, zm, z2 = (z + 1) % 4, (z + 3) % 4, (z + 2) % 4
    root = h == y // 2
    hub = x == z
    far = jnp.logical_not(hub)
    twin = (c, z * 2 + 1 - h)

    def part(name, lo):
        first, rows = ROWS[name]
        return t1[pl.ds(first + lo * rows, rows), :]

    def table(name):
        return part(name, 0), part(name, 1)

    def local(src, dst, sem):
        return pltpu.make_async_copy(src, dst, sem)

    def remote(src, dst, send, recv, to):
        return pltpu.make_async_remote_copy(
            src_ref=src, dst_ref=dst, send_sem=send, recv_sem=recv, device_id=to, device_id_type=MESH
        )

    def clus_group(src_of, dst, send_sem, recv_sem):
        def body(i, carry):
            to = lax.rem(c + i, 16)
            remote(src_of(to), dst.at[c], send_sem, recv_sem, (to, k)).start()
            return carry

        lax.fori_loop(1, 16, body, 0)
        local(src_of(c), dst.at[c], recv_sem).start()

    def col_group(src_of, dst, send_sem, recv_sem):
        for i in range(1, 8):
            to = (k + i) % 8
            remote(src_of(to), dst.at[k], send_sem, recv_sem, (c, to)).start()
        local(src_of(k), dst.at[k], recv_sem).start()

    bar = pltpu.get_barrier_semaphore()

    def greet(i, carry):
        pl.semaphore_signal(bar, inc=1, device_id=(lax.rem(c + i, 16), k), device_id_type=MESH)
        return carry

    lax.fori_loop(1, 16, greet, 0)
    for i in range(1, 8):
        pl.semaphore_signal(bar, inc=1, device_id=(c, (k + i) % 8), device_id_type=MESH)
    loads = [
        local(t1_hbm, t1, lsem.at[0]),
        local(phi_ref, phi, lsem.at[1]),
        local(ty_hbm, ty, lsem.at[2]),
        local(selc_hbm, selc, lsem.at[3]),
    ]
    for copy in loads:
        copy.start()
    for i in range(2):
        for j in range(4):
            keep = pat_ref[i, j].astype(f32).astype(bf16)
            at_rows, at_cols = pl.ds(i * B, B), pl.ds(j * B, B)
            masked[at_rows, at_cols] = dens_ref[at_rows, at_cols] * keep
    wd[y] = masked[0:B, :]
    for j in range(4):
        at_rows = pl.ds(j * B, B)
        wm[x, at_rows, :] = margin_ref[at_rows, :] * ovl_ref[0, j].astype(f32).astype(bf16)
    loads[0].wait()
    lines = dot3(table("tz"), split2(rest_ref[...].reshape(512, G)), NT)
    for i in range(2):
        for j in range(4):
            s1[:, i * 4 + j, :] = lines[i * 128 : (i + 1) * 128, j * 128 : (j + 1) * 128]
    loads[1].wait()
    pl.semaphore_wait(bar, 22)

    to_y = [(x * 4 + (y + i) % 4, k) for i in range(1, 4)]
    to_x = [((x + i) % 4 * 4 + y, k) for i in range(1, 4)]
    rows_out = [remote(wd.at[y], wd.at[y], wd_s.at[i], wd_r.at[y], to) for i, to in enumerate(to_y)]
    cols_out = [remote(wm.at[x], wm.at[x], wm_s.at[i], wm_r.at[x], to) for i, to in enumerate(to_x)]
    for copy in rows_out:
        copy.start()

    first = 2 * (y % 2)

    def own_part(g):
        return phi.at[pl.ds(first, 2), :, pl.ds(pl.multiple_of(g * CH, CH), CH)]

    to_send = []

    def send(when, src, dst, recv, to):
        index = len(to_send)
        copy = remote(src, dst, ssem.at[index], recv, to)
        to_send.append((when, copy))
        pl.when(when)(copy.start)

    def share(dist):
        pair, count = FIRST[0], SHARE[0]
        for d in range(1, 4):
            pair = jnp.where(dist == d, FIRST[d], pair)
            count = jnp.where(dist == d, SHARE[d], count)
        return pair, count

    my_pair, my_count = share((x - z) % 4)

    def batch(i):
        for turn in range(2):
            for up in (True, False):
                half = turn if up else 1 - turn
                slot = 0 if up else 1
                send(
                    root & (i < my_count), own_part(jnp.minimum(2 * (my_pair + i) + half, NCH - 1)),
                    relay.at[slot, i], tsem.at[slot, i], (c, (zp if up else zm) * 2 + half),
                )

    batch(0)
    batch(1)

    clus_group(lambda to: s1.at[pl.ds(pl.multiple_of(to * 8, 8), 8)], x1, a1_s, a1_r)
    for copy in cols_out:
        copy.start()

    hub_root = hub & root

    @pl.when(hub_root)
    def _():
        def body(g, carry):
            remote(own_part(g), rblk.at[g], fsem.at[g], rsem.at[g], twin).start()
            local(own_part(g), rblk.at[g], rsem.at[g]).start()
            return carry

        lax.fori_loop(0, NCH, body, 0)

    row_id = lax.broadcasted_iota(jnp.int32, (G, G), 0)
    col_id = lax.broadcasted_iota(jnp.int32, (G, G), 1)

    def wave(freq, axis):
        signed = jnp.where(freq < G // 2, freq, freq - G).astype(f32)
        scaled = signed * (2.0 * math.pi) / jnp.full(freq.shape, len_ref[axis], f32)
        return scaled * scaled

    flat = wave(row_id, 0) + wave(col_id, 1)
    for out, kz in ((ga, me), (gb, jnp.where(me == 0, 128, me))):
        kz = jnp.full((G, G), kz, jnp.int32)
        anchor = (row_id == 0) & (col_id == 0) & (kz == 0)
        out[...] = jnp.where(anchor, 0.0, four_pi / jnp.where(anchor, 1.0, flat + wave(kz, 2)))

    stages = []
    for i in range(MOST + 1):
        if i < MOST:
            stages += [(0, i), (1, i)]
        if i:
            stages.append((2, i - 1))
    for slot, i in stages:
        plane = (zm, zp, z2)[slot]
        pair, count = share((x - plane) % 4)
        have = i < count

        @pl.when(have)
        def _():
            local(relay.at[slot, i], relay.at[slot, i], tsem.at[slot, i]).wait()

        if slot == 1 and i + 2 < MOST:
            batch(i + 2)
        if slot == 0:
            send(have & (h == 0), relay.at[0, i], relay.at[2, i], tsem.at[2, i], (c, zp * 2))
        if slot == 1:
            send(have & (h == 1), relay.at[1, i], relay.at[2, i], tsem.at[2, i], (c, zm * 2 + 1))
        here = plane == x
        g = jnp.minimum(2 * (pair + i) + h, NCH - 1)
        send(have & here, relay.at[slot, i], rblk.at[g], rsem.at[g], twin)
        send(have & jnp.logical_not(here), relay.at[slot, i], rblk.at[g], rsem.at[g], (plane * 4 + y, k))

        @pl.when(have & here)
        def _():
            local(relay.at[slot, i], rblk.at[g], rsem.at[g]).start()

    local(x1, x1, a1_r).wait()
    col_group(lambda to: x1.at[:, to], r1, a2_s, a2_r)

    def pair_at(t):
        i, line = t // 3, t % 3
        return jnp.where(t == 15, 10, jnp.where(line == 0, i, jnp.where(line == 1, 5 + i, 11 + i)))

    def passed_on(pair):
        g = 2 * pair + h
        return far & (pair >= 5), remote(rblk.at[g], rblk.at[g], fsem.at[g], rsem.at[g], twin)

    def step(t, carry):
        @pl.when(t < 16)
        def _():
            pair = pair_at(t)
            g = 2 * pair + h
            local(rblk.at[g], rblk.at[g], rsem.at[g]).wait()
            when, copy = passed_on(pair)
            pl.when(when)(copy.start)

        @pl.when(t > 0)
        def _():
            pair = pair_at(t - 1)
            g = 2 * pair + 1 - h
            local(rblk.at[g], rblk.at[g], rsem.at[g]).wait()
            cells = pl.ds(pl.multiple_of(pair * 2 * CH, 2 * CH), 2 * CH)
            values = phi[:, :, cells].reshape(4 * B, 2 * CH)
            for i in range(2):
                lifted = dot(masked[i * B : (i + 1) * B, :], values)
                for j in range(2):
                    basis = rblk[2 * pair + j, i].astype(f32)
                    summed = jnp.sum(basis * lifted[:, j * CH : (j + 1) * CH], axis=0, keepdims=True)
                    rp[pair // 2, pl.ds(i * 4 + pair % 2 * 2 + j, 1), :] = summed

        return carry

    lax.fori_loop(0, 17, step, 0)
    for l in range(8):
        away = l != k

        @pl.when(away)
        def _():
            remote(rp.at[l], rq.at[k], q_s.at[l], q_r.at[k], (c, l)).start()

        @pl.when(jnp.logical_not(away))
        def _():
            local(rp.at[l], rq.at[k], q_r.at[k]).start()

    for i in range(1, 4):
        ny, nx = (y + i) % 4, (x + i) % 4
        local(wd.at[ny], wd.at[ny], wd_r.at[ny]).wait()
        local(wm.at[nx], wm.at[nx], wm_r.at[nx]).wait()

    def tile_step(t, carry):
        tt[t % 4 // 2, t // 4, t % 2] = dot(wd[t // 4], wm[t % 4])
        return carry

    lax.fori_loop(0, 16, tile_step, 0)
    swap = remote(tt.at[1 - h], trx, tw_s, tw_r, twin)
    swap.start()
    for l in range(8):
        local(rq.at[l], rq.at[l], q_r.at[l]).wait()
    rho = jnp.sum(rq[...], axis=0)

    pad[...] = jnp.zeros_like(pad)
    pad[0:8, 0:128] = rho
    pad[8:16, 128:256] = rho
    for copy in loads[2:]:
        copy.wait()
    v1[...] = dot3(table("tq"), split2(pad[...]), NT).reshape(ND, 1, 128)
    clus_group(lambda to: v1.at[pl.ds(to * 8, 8)], xv, g1_s, g1_r)

    local(xv, xv, g1_r).wait()
    col_group(lambda to: xv.at[:, to], rv, g2_s, g2_r)

    lane = lax.broadcasted_iota(jnp.int32, (1, 1, 128), 2) // 32
    low = lax.broadcasted_iota(jnp.int32, (1, 8, 1), 1) < 4
    local(r1, r1, a2_r).wait()
    for kk in range(2):
        got = [r1[kk * 4 + k4] for k4 in range(4)]
        for p4 in range(4):
            tile = got[p4]
            for k4 in range(4):
                if k4 != p4:
                    turned = pltpu.roll(got[k4], (k4 - p4) % 4 * 32, 2)
                    tile = jnp.where(lane == k4, turned, tile)
            pairs = tile.reshape(8, 2, 8, 128)
            even, odd = pairs[:, 0], pairs[:, 1]
            at_rows, at_cols = pl.ds(p4 * 64, 64), pl.ds(kk * 128, 128)
            xa[at_rows, at_cols] = jnp.where(low, even, pltpu.roll(odd, 4, 1)).reshape(64, 128)
            xa[pl.ds(256 + p4 * 64, 64), at_cols] = jnp.where(low, pltpu.roll(even, 4, 1), odd).reshape(64, 128)

    def block_of(row):
        return row % 16 * 2 + row // 16

    spot = lax.broadcasted_iota(jnp.int32, (1, 32), 1)
    x_cell = jnp.zeros((1, 32), jnp.int32)
    order = lax.broadcasted_iota(jnp.int32, (32, G), 0)
    x_pick = jnp.zeros((32, G), jnp.int32)
    for row in range(32):
        cell = own_ref[block_of(row)] * 16 + block_of(row) % 16
        x_cell = jnp.where(spot == row, cell, x_cell)
        x_pick = jnp.where(order == row, cell, x_pick)
    row_x = x_of_row(lax.broadcasted_iota(jnp.int32, (G, 1), 0))
    sits = (row_x == x_cell).astype(f32).astype(bf16)
    lane_id = lax.broadcasted_iota(jnp.int32, (16, 128), 1)
    upper = lax.broadcasted_iota(jnp.int32, (16, 128), 0) // 8
    valid_lane = lane_id % 32 // 4 == upper
    swap.wait_recv()
    side = y // 2

    def to_collect(i):
        target = 2 * h + i
        stays = (target == z) & (side == h)
        return stays, remote(zs.at[i], zr.at[z], zs_s.at[i], zr_r.at[z], (c, target * 2 + side))

    for i in range(2):
        for j in range(4):
            zs[i, j] = (tt[h, j, i] + trx[j, i]).astype(bf16)
        stays, copy = to_collect(i)
        pl.when(jnp.logical_not(stays))(copy.start)

        @pl.when(stays)
        def _():
            local(zs.at[i], zr.at[z], zr_r.at[z]).start()

    local(rv, rv, g2_r).wait()
    spread = []
    for half in range(2):
        acc = None
        for l4 in range(4):
            values = rv[half * 4 + l4].reshape(16, 128)
            if l4:
                values = pltpu.roll(values, l4 * 32, 1)
            acc = values if acc is None else jnp.where(lane_id // 32 == l4, values, acc)
        spread.append(acc)
    for i in range(2):
        rows = []
        for il in range(2):
            offset = i * 8 + il * 4
            halves = []
            for acc in spread:
                low_row = pltpu.roll(acc, (128 - offset) % 128, 1) if offset else acc
                high_row = pltpu.roll(acc, (132 - offset) % 128, 1) if offset != 4 else acc
                halves.append(jnp.where(valid_lane, jnp.where(upper == 0, low_row, high_row), 0.0))
            rows.append(jnp.concatenate(halves, axis=1))
        hi, lo = split2(jnp.concatenate(rows, axis=0))
        xa[pl.ds(i * G, G), :] = xa[pl.ds(i * G, G), :] + (dot(sits, hi) + dot(sits, lo))

    ty_pair = ty[0:G, :], ty[G : 2 * G, :]
    big[...] = dot3(split2(xa[...]), ty_pair)
    wx = table("wx")
    fields = []
    for i in range(2):
        quad = dot3(wx, split2(big[pl.ds(i * G, G), :]))
        fields.append((quad[:G, :G] - quad[G:, G:], -(quad[G:, :G] + quad[:G, G:])))
    (a_re, a_im), (b_re, b_im) = fields
    xa[0:G, :] = ga[...] * a_re - gb[...] * b_im
    xa[G : 2 * G, :] = ga[...] * a_im + gb[...] * b_re
    back = dot3(split2(xa[...]), ty_pair)
    big[0:G, 0:G] = back[:G, :G] - back[G:, G:]
    big[0:G, G : 2 * G] = back[:G, G:] + back[G:, :G]
    quad = dot3(table("wi"), split2(big[0:G, :]))
    xa[0:G, :] = quad[:G, :G] - quad[G:, G:]
    xa[G : 2 * G, :] = quad[:G, G:] + quad[G:, :G]

    row_of = x_of_row(lax.broadcasted_iota(jnp.int32, (32, G), 1))
    pick = (row_of == x_pick).astype(f32).astype(bf16)
    line = lax.broadcasted_iota(jnp.int32, (32, G), 1)
    valid = line % 32 // 4 == order % 16 // 8
    rows = []
    for i in range(2):
        hi, lo = split2(xa[pl.ds(i * G, G), :])
        here = jnp.where(valid, dot(pick, hi) + dot(pick, lo), 0.0)
        rows += [here[0:16], here[16:32]]
    hi, lo = split2(jnp.concatenate(rows, axis=1))
    packed = dot(hi, selc[...]) + dot(lo, selc[...])
    for i in range(16):
        s3[i] = packed[i : i + 1, :]
    clus_group(lambda to: s3.at[to], x3, p1_s, p1_r)

    for kk in range(2):
        tiles = []
        at_cols = pl.ds(kk * 128, 128)
        for p4 in range(4):
            re = xa[pl.ds(p4 * 64, 64), at_cols].reshape(8, 8, 128)
            im = xa[pl.ds(256 + p4 * 64, 64), at_cols].reshape(8, 8, 128)
            even = jnp.where(low, re, pltpu.roll(im, 4, 1))
            odd = jnp.where(low, pltpu.roll(re, 4, 1), im)
            tiles.append(jnp.stack([even, odd], axis=1).reshape(16, 8, 128))
        for k4 in range(4):
            tile = tiles[k4]
            for p4 in range(4):
                if p4 != k4:
                    tile = jnp.where(lane == p4, pltpu.roll(tiles[p4], (p4 - k4) % 4 * 32, 2), tile)
            s2[:, kk * 4 + k4] = tile
    clus_group(lambda to: s2.at[to], x2, b1_s, b1_r)
    local(x3, x3, p1_r).wait()
    col_group(lambda to: x3, r3, p2_s, p2_r)

    collects = h == side

    def to_owner(j):
        ny = (y + j) % 4
        return remote(ys.at[ny], yr.at[y % 2], ys_s.at[j - 1], yr_r.at[y % 2], (x * 4 + ny, k))

    @pl.when(collects)
    def _():
        for i in range(4):
            local(zr.at[i], zr.at[i], zr_r.at[i]).wait()
        for j in range(4):
            total = zr[0, j].astype(f32) + zr[1, j].astype(f32) + (zr[2, j].astype(f32) + zr[3, j].astype(f32))
            ys[j] = total.astype(bf16)
        for j in range(1, 4):
            to_owner(j).start()
        local(ys.at[y], yr.at[y % 2], yr_r.at[y % 2]).start()

    local(r3, r3, p2_r).wait()
    arrived = split2(r3[...].reshape(ND, 128))
    both = dot3(arrived, table("tp"), TN)
    rho_pot = both[:64, :128] + both[64:, 128:]
    for i in range(2):
        for g in range(NCH):
            at_row = i * 32 + g
            scaled = rblk[g, i].astype(f32) * rho_pot[at_row : at_row + 1, :]
            wt[pl.ds(i * B, B), pl.ds(g * CH, CH)] = scaled.astype(bf16)
    for j in range(4):
        if j == 2:
            local(x2, x2, b1_r).wait()
            col_group(lambda to: x2.at[:, to], r2, b2_s, b2_r)
        for i in range(2):
            block_sum = dot(wt[pl.ds(i * B, B), :], phi[j], NT)
            har_ref[pl.ds(i * B, B), pl.ds(j * B, B)] = (block_sum * pat_ref[i, j].astype(f32)).astype(bf16)

    done = [local(har_ref, har_out, osem.at[0])]
    done[0].start()
    local(r2, r2, b2_r).wait()
    lines_back = r2[...].reshape(ND, 8, 128)
    tzi = table("tzi")
    for j in range(4):
        got = jnp.concatenate([lines_back[:, j, :], lines_back[:, 4 + j, :]], axis=0)
        pot_ref[pl.ds(j * 4, 4)] = dot3(split2(got), tzi, TN).reshape(4, 32, G)

    done.append(local(pot_ref, pot_out, osem.at[1]))
    done[1].start()
    for i in range(2):
        local(yr.at[i], yr.at[i], yr_r.at[i]).wait()
        prod_ref[:, pl.ds(i * B, B)] = yr[i] * keep_ref[0, i].astype(f32).astype(bf16)

    done.append(local(prod_ref, prod_out, osem.at[2]))
    done[2].start()

    for copy in rows_out + cols_out + [swap]:
        copy.wait_send()
    for i in range(2):
        stays, copy = to_collect(i)
        pl.when(jnp.logical_not(stays))(copy.wait_send)

    @pl.when(collects)
    def _():
        for j in range(1, 4):
            to_owner(j).wait_send()

    for when, copy in to_send:
        pl.when(when)(copy.wait_send)

    def leave(g, carry):
        remote(rblk.at[g], rblk.at[g], fsem.at[g], rsem.at[g], twin).wait_send()
        return carry

    @pl.when(hub_root)
    def _():
        lax.fori_loop(0, NCH, leave, 0)

    @pl.when(far)
    def _():
        lax.fori_loop(5, 16, lambda pair, carry: leave(2 * pair + h, carry), 0)

    for l in range(8):

        @pl.when(l != k)
        def _():
            remote(rp.at[l], rq.at[k], q_s.at[l], q_r.at[k], (c, l)).wait_send()

    for dst, sem in ((x1, a1_s), (xv, g1_s), (x3, p1_s), (x2, b1_s)):
        rest_of = dst.at[pl.ds(0, 15)]
        local(rest_of, rest_of, sem).wait()
    for dst, sem in ((r1, a2_s), (rv, g2_s), (r3, p2_s), (r2, b2_s)):
        rest_of = dst.at[pl.ds(0, 7)]
        local(rest_of, rest_of, sem).wait()
    for copy in done:
        copy.wait()


def hand_over(*refs):
    arrays, outs, held, sem = refs[:3], refs[3:6], refs[6:9], refs[9]
    into = [pltpu.make_async_copy(arrays[i], held[i], sem.at[i]) for i in range(3)]
    away = [pltpu.make_async_copy(held[i], outs[i], sem.at[3 + i]) for i in range(3)]
    for copy in into:
        copy.start()
    for i in (2, 0, 1):
        into[i].wait()
        away[i].start()
    for copy in away:
        copy.wait()


def final_copy(arrays):
    hbm = pl.BlockSpec(memory_space=pl.ANY)
    return pl.pallas_call(
        hand_over,
        out_shape=tuple(jax.ShapeDtypeStruct(a.shape, a.dtype) for a in arrays),
        in_specs=[hbm] * 3,
        out_specs=(hbm,) * 3,
        scratch_shapes=[pltpu.VMEM(a.shape, a.dtype) for a in arrays] + [pltpu.SemaphoreType.DMA((6,))],
        compiler_params=pltpu.CompilerParams(vmem_limit_bytes=62 << 20),
        cost_estimate=pl.CostEstimate(flops=0, bytes_accessed=4 << 20, transcendentals=0),
    )(*arrays)


def main_call(density, pattern, margin, ovl, keep, basis, rest, slab_owner, lengths):
    t1, ty, selc = tables()
    vmem = pl.BlockSpec(memory_space=pltpu.VMEM)
    smem = pl.BlockSpec(memory_space=pltpu.SMEM)
    hbm = pl.BlockSpec(memory_space=pl.ANY)
    V = pltpu.VMEM
    D = pltpu.SemaphoreType.DMA
    return pl.pallas_call(
        kernel,
        out_shape=(
            jax.ShapeDtypeStruct((16, 32, G), f32),
            jax.ShapeDtypeStruct((512, 1024), bf16),
            jax.ShapeDtypeStruct((B, 2 * B), bf16),
        ),
        in_specs=[smem] * 4 + [vmem, smem, vmem, hbm, vmem, hbm, hbm, hbm],
        out_specs=(hbm, hbm, hbm),
        scratch_shapes=[
            V((16, 32, G), f32),
            V((512, 1024), bf16),
            V((B, 2 * B), bf16),
            V((4, B, 4096), bf16),
            V((NCH, 2, B, CH), bf16),
            V((3, MOST, 2, B, CH), bf16),
            V((512, 1024), bf16),
            V((512, 4096), bf16),
            V((T1_ROWS, G), bf16),
            V((2 * G, 2 * G), bf16),
            V((1024, 128), bf16),
            V((ND, 8, 128), f32),
            V((16, 8, 8, 128), f32),
            V((8, 16, 8, 128), f32),
            V((16, 8, 8, 128), f32),
            V((16, 8, 8, 128), f32),
            V((8, 16, 8, 128), f32),
            V((16, 1, 128), f32),
            V((16, 1, 128), f32),
            V((8, 16, 1, 128), f32),
            V((ND, 1, 128), f32),
            V((16, 8, 1, 128), f32),
            V((8, 16, 1, 128), f32),
            V((8, 8, 128), f32),
            V((8, 8, 128), f32),
            V((128, 2 * 128), f32),
            V((2 * G, G), f32),
            V((G, G), f32),
            V((G, G), f32),
            V((2 * G, 2 * G), f32),
            V((4, B, 1024), bf16),
            V((4, 1024, B), bf16),
            V((2, 4, 2, B, B), f32),
            V((4, 2, B, B), f32),
            V((2, 4, B, B), bf16),
            V((4, 4, B, B), bf16),
            V((4, B, B), bf16),
            V((2, B, B), bf16),
            D((5,)),
            D((3, MOST)),
            D((NCH,)),
            D((64,)),
            D((NCH,)),
            D((8,)),
            D((8,)),
            *([D(())] * 16),
            D((3,)),
            D((4,)),
            D((3,)),
            D((4,)),
            D(()),
            D(()),
            D((2,)),
            D((4,)),
            D((3,)),
            D((2,)),
            D((3,)),
        ],
        compiler_params=pltpu.CompilerParams(
            collective_id=0, has_side_effects=True, vmem_limit_bytes=58 << 20
        ),
        cost_estimate=pl.CostEstimate(flops=12 * 10**9, bytes_accessed=24 << 20, transcendentals=0),
    )(pattern, lengths, ovl, keep, margin, slab_owner, density, basis, rest, t1, ty, selc)


def per_device(
    density, dens_pattern, margin_window, ovl_pattern, keep_mask, basis_values, rest_density,
    slab_owner, cell_lengths,
):
    return final_copy(main_call(
        density, dens_pattern, margin_window, ovl_pattern.T, keep_mask, basis_values,
        rest_density, slab_owner, cell_lengths,
    ))


def solution(mesh):
    return jax.shard_map(
        per_device,
        mesh=mesh,
        in_specs=(
            P("clus", "col"),
            P("clus", "col"),
            P("col", "clus"),
            P("col", "clus"),
            P("clus", "col"),
            P("col", None, None),
            P("clus", "col", None),
            P(),
            P(),
        ),
        out_specs=(P("clus", "col", None), P("clus", "col"), P("clus", "col")),
        check_vma=False,
    )
```

time: 123 us -> 105 us (0.85)
  local copies, waits for them, and re-layouts: 9.63 us -> 0 us
  Pallas kernels: 111 us -> 104 us
    pallas_call x1 -> x2, Pallas kernels: 111 us -> 104 us  [the longest x1 101 us: main_call(): pl.pallas_call(kernel, out_shape=(jax.ShapeDtypeStruct((16, 32, G), f32),...]
    unnamed x4 -> x0, local copies, waits for them, and re-layouts: 7.12 us -> none
    reshape x3 -> x0, local copies, waits for them, and re-layouts: 2.25 us -> none  [the longest x2 1.45 us: main_call(): order = slab_owner.reshape(16, 2).T.reshape(32, 1)]
where the time goes in v2:
time: 105 us
  Pallas kernels  104 us (99%)
    pallas_call x1, Pallas kernels, main_call(): pl.pallas_call(kernel, out_shape=(jax.ShapeDtypeStruct((16, 32, G), f32),...  101 us
    pallas_call x1, Pallas kernels, final_copy(): pl.pallas_call(hand_over, out_shape=tuple((jax.ShapeDtypeStruct(a.shape,...  2.71 us

profile of v2, /device:TPU:1, one launch (start us, length us, event | category | flops | bytes accessed | tf_op | source)
XLA Modules:
  0.0 104.5 jit_solution(6762068467257854252)
XLA Ops:
  0.6 101.2 %shard_map.139 = (f32[16,32,256]{2,1,0:T(8,128)}, bf16[512,1024]{1,0:T(8,128)(2,1)}, bf16[256,512]{1,0:T(8,128)(2,1)}) custom-call(s32[2,4]{1,0:T(2,128)} %pat_ref.1, f32[3]{0:T(128)} %len_ref.1, s32[1,4]{1,0:T(1,128)} %bitcast.1, s32[1,2]{1,0:T(1,128)} %keep_ref.1, bf16[1024,256]{1,0:T(8,128)(2,1)} %margin_ref.1, s32[32]{0:T(128)} %own_ref.1, ...), custom_call_target="tpu_custom_call" | custom-call | flops 12000000000 | bytes 25165824 | tf_op jit(solution)/shard_map/pallas_call | solution.py:610
  101.8 2.7 %shard_map.140 = (f32[16,32,256]{2,1,0:T(8,128)}, bf16[512,1024]{1,0:T(8,128)(2,1)}, bf16[256,512]{1,0:T(8,128)(2,1)}) custom-call(f32[16,32,256]{2,1,0:T(8,128)} %get-tuple-element.6.refs_0_, bf16[512,1024]{1,0:T(8,128)(2,1)} %get-tuple-element.7.refs_1_, bf16[256,512]{1,0:T(8,128)(2,1)} %get-tuple-element.8.refs_2_), custom_call_target="tpu_custom_call" | custom-call | bytes 4194304 | tf_op jit(solution)/shard_map/pallas_call | solution.py:592

commit v3 on v2

--- a/solution.py
+++ b/solution.py
@@ -17,9 +17,10 @@
 ND = 128
 CH = 128
 NCH = 32
-SHARE = (5, 5, 1, 5)
-FIRST = (0, 5, 10, 11)
-MOST = 5
+SHARE = (8, 4, 0, 4)
+FIRST = (0, 8, 12, 12)
+MOST = 8
+ARRIVE = [FIRST[d] + i for i in range(MOST) for d in (0, 1, 3, 2) if i < SHARE[d]]
 four_pi = 4.0 * math.pi
 f32 = jnp.float32
 bf16 = jnp.bfloat16
@@ -162,6 +163,43 @@
     ]
     for copy in loads:
         copy.start()
+    pl.semaphore_wait(bar, 22)
+
+    first = 2 * (y % 2)
+
+    def own_part(g):
+        return phi_ref.at[pl.ds(first, 2), :, pl.ds(pl.multiple_of(g * CH, CH), CH)]
+
+    to_send = []
+
+    def send(when, src, dst, recv, to):
+        index = len(to_send)
+        copy = remote(src, dst, ssem.at[index], recv, to)
+        to_send.append((when, copy))
+        pl.when(when)(copy.start)
+
+    def share(dist):
+        pair, count = FIRST[0], SHARE[0]
+        for d in range(1, 4):
+            pair = jnp.where(dist == d, FIRST[d], pair)
+            count = jnp.where(dist == d, SHARE[d], count)
+        return pair, count
+
+    my_pair, my_count = share((x - z) % 4)
+
+    def batch(i):
+        for turn in range(2):
+            for up in (True, False):
+                half = turn if up else 1 - turn
+                slot = 0 if up else 1
+                send(
+                    root & (i < my_count), own_part(jnp.minimum(2 * (my_pair + i) + half, NCH - 1)),
+                    relay.at[slot, i], tsem.at[slot, i], (c, (zp if up else zm) * 2 + half),
+                )
+
+    batch(0)
+    batch(1)
+
     for i in range(2):
         for j in range(4):
             keep = pat_ref[i, j].astype(f32).astype(bf16)
@@ -171,14 +209,6 @@
     for j in range(4):
         at_rows = pl.ds(j * B, B)
         wm[x, at_rows, :] = margin_ref[at_rows, :] * ovl_ref[0, j].astype(f32).astype(bf16)
-    loads[0].wait()
-    lines = dot3(table("tz"), split2(rest_ref[...].reshape(512, G)), NT)
-    for i in range(2):
-        for j in range(4):
-            s1[:, i * 4 + j, :] = lines[i * 128 : (i + 1) * 128, j * 128 : (j + 1) * 128]
-    loads[1].wait()
-    pl.semaphore_wait(bar, 22)
-
     to_y = [(x * 4 + (y + i) % 4, k) for i in range(1, 4)]
     to_x = [((x + i) % 4 * 4 + y, k) for i in range(1, 4)]
     rows_out = [remote(wd.at[y], wd.at[y], wd_s.at[i], wd_r.at[y], to) for i, to in enumerate(to_y)]
@@ -186,41 +216,11 @@
     for copy in rows_out:
         copy.start()
 
-    first = 2 * (y % 2)
-
-    def own_part(g):
-        return phi.at[pl.ds(first, 2), :, pl.ds(pl.multiple_of(g * CH, CH), CH)]
-
-    to_send = []
-
-    def send(when, src, dst, recv, to):
-        index = len(to_send)
-        copy = remote(src, dst, ssem.at[index], recv, to)
-        to_send.append((when, copy))
-        pl.when(when)(copy.start)
-
-    def share(dist):
-        pair, count = FIRST[0], SHARE[0]
-        for d in range(1, 4):
-            pair = jnp.where(dist == d, FIRST[d], pair)
-            count = jnp.where(dist == d, SHARE[d], count)
-        return pair, count
-
-    my_pair, my_count = share((x - z) % 4)
-
-    def batch(i):
-        for turn in range(2):
-            for up in (True, False):
-                half = turn if up else 1 - turn
-                slot = 0 if up else 1
-                send(
-                    root & (i < my_count), own_part(jnp.minimum(2 * (my_pair + i) + half, NCH - 1)),
-                    relay.at[slot, i], tsem.at[slot, i], (c, (zp if up else zm) * 2 + half),
-                )
-
-    batch(0)
-    batch(1)
-
+    loads[0].wait()
+    lines = dot3(table("tz"), split2(rest_ref[...].reshape(512, G)), NT)
+    for i in range(2):
+        for j in range(4):
+            s1[:, i * 4 + j, :] = lines[i * 128 : (i + 1) * 128, j * 128 : (j + 1) * 128]
     clus_group(lambda to: s1.at[pl.ds(pl.multiple_of(to * 8, 8), 8)], x1, a1_s, a1_r)
     for copy in cols_out:
         copy.start()
@@ -250,6 +250,7 @@
         anchor = (row_id == 0) & (col_id == 0) & (kz == 0)
         out[...] = jnp.where(anchor, 0.0, four_pi / jnp.where(anchor, 1.0, flat + wave(kz, 2)))
 
+    loads[1].wait()
     stages = []
     for i in range(MOST + 1):
         if i < MOST:
@@ -283,13 +284,31 @@
     local(x1, x1, a1_r).wait()
     col_group(lambda to: x1.at[:, to], r1, a2_s, a2_r)
 
+    def block_of(row):
+        return row % 16 * 2 + row // 16
+
+    spot = lax.broadcasted_iota(jnp.int32, (1, 32), 1)
+    x_cell = jnp.zeros((1, 32), jnp.int32)
+    order = lax.broadcasted_iota(jnp.int32, (32, G), 0)
+    x_pick = jnp.zeros((32, G), jnp.int32)
+    for row in range(32):
+        cell = own_ref[block_of(row)] * 16 + block_of(row) % 16
+        x_cell = jnp.where(spot == row, cell, x_cell)
+        x_pick = jnp.where(order == row, cell, x_pick)
+    row_x = x_of_row(lax.broadcasted_iota(jnp.int32, (G, 1), 0))
+    sits = (row_x == x_cell).astype(f32).astype(bf16)
+    row_of = x_of_row(lax.broadcasted_iota(jnp.int32, (32, G), 1))
+    pick = (row_of == x_pick).astype(f32).astype(bf16)
+
     def pair_at(t):
-        i, line = t // 3, t % 3
-        return jnp.where(t == 15, 10, jnp.where(line == 0, i, jnp.where(line == 1, 5 + i, 11 + i)))
+        pair = ARRIVE[0]
+        for i in range(1, 16):
+            pair = jnp.where(t == i, ARRIVE[i], pair)
+        return pair
 
     def passed_on(pair):
         g = 2 * pair + h
-        return far & (pair >= 5), remote(rblk.at[g], rblk.at[g], fsem.at[g], rsem.at[g], twin)
+        return far & (pair >= SHARE[0]), remote(rblk.at[g], rblk.at[g], fsem.at[g], rsem.at[g], twin)
 
     def step(t, carry):
         @pl.when(t < 16)
@@ -372,22 +391,27 @@
             xa[at_rows, at_cols] = jnp.where(low, even, pltpu.roll(odd, 4, 1)).reshape(64, 128)
             xa[pl.ds(256 + p4 * 64, 64), at_cols] = jnp.where(low, pltpu.roll(even, 4, 1), odd).reshape(64, 128)
 
-    def block_of(row):
-        return row % 16 * 2 + row // 16
-
-    spot = lax.broadcasted_iota(jnp.int32, (1, 32), 1)
-    x_cell = jnp.zeros((1, 32), jnp.int32)
-    order = lax.broadcasted_iota(jnp.int32, (32, G), 0)
-    x_pick = jnp.zeros((32, G), jnp.int32)
-    for row in range(32):
-        cell = own_ref[block_of(row)] * 16 + block_of(row) % 16
-        x_cell = jnp.where(spot == row, cell, x_cell)
-        x_pick = jnp.where(order == row, cell, x_pick)
-    row_x = x_of_row(lax.broadcasted_iota(jnp.int32, (G, 1), 0))
-    sits = (row_x == x_cell).astype(f32).astype(bf16)
     lane_id = lax.broadcasted_iota(jnp.int32, (16, 128), 1)
     upper = lax.broadcasted_iota(jnp.int32, (16, 128), 0) // 8
     valid_lane = lane_id % 32 // 4 == upper
+    ty_pair = ty[0:G, :], ty[G : 2 * G, :]
+    wx, wi = table("wx"), table("wi")
+
+    def spectrum(tab, lines):
+        parts = []
+        for values in lines:
+            quad = dot3(tab, split2(values))
+            parts.append((quad[:G, :G] - quad[G:, G:], -(quad[G:, :G] + quad[:G, G:])))
+        (a_re, a_im), (b_re, b_im) = parts
+        return ga[...] * a_re - gb[...] * b_im, ga[...] * a_im + gb[...] * b_re
+
+    big[...] = dot3(split2(xa[...]), ty_pair)
+    xa[0:G, :], xa[G : 2 * G, :] = spectrum(wx, (big[0:G, :], big[G : 2 * G, :]))
+    at_x = tuple(dot(tab, sits).astype(bf16) for tab in wx)
+    to_x_rows = tuple(
+        jnp.concatenate([dot(pick, tab[:G]), dot(pick, tab[G:])], axis=0).astype(bf16) for tab in wi
+    )
+
     swap.wait_recv()
     side = y // 2
 
@@ -416,6 +440,7 @@
                 values = pltpu.roll(values, l4 * 32, 1)
             acc = values if acc is None else jnp.where(lane_id // 32 == l4, values, acc)
         spread.append(acc)
+    lines_y = []
     for i in range(2):
         rows = []
         for il in range(2):
@@ -426,34 +451,23 @@
                 high_row = pltpu.roll(acc, (132 - offset) % 128, 1) if offset != 4 else acc
                 halves.append(jnp.where(valid_lane, jnp.where(upper == 0, low_row, high_row), 0.0))
             rows.append(jnp.concatenate(halves, axis=1))
-        hi, lo = split2(jnp.concatenate(rows, axis=0))
-        xa[pl.ds(i * G, G), :] = xa[pl.ds(i * G, G), :] + (dot(sits, hi) + dot(sits, lo))
-
-    ty_pair = ty[0:G, :], ty[G : 2 * G, :]
-    big[...] = dot3(split2(xa[...]), ty_pair)
-    wx = table("wx")
-    fields = []
-    for i in range(2):
-        quad = dot3(wx, split2(big[pl.ds(i * G, G), :]))
-        fields.append((quad[:G, :G] - quad[G:, G:], -(quad[G:, :G] + quad[:G, G:])))
-    (a_re, a_im), (b_re, b_im) = fields
-    xa[0:G, :] = ga[...] * a_re - gb[...] * b_im
-    xa[G : 2 * G, :] = ga[...] * a_im + gb[...] * b_re
-    back = dot3(split2(xa[...]), ty_pair)
-    big[0:G, 0:G] = back[:G, :G] - back[G:, G:]
-    big[0:G, G : 2 * G] = back[:G, G:] + back[G:, :G]
-    quad = dot3(table("wi"), split2(big[0:G, :]))
-    xa[0:G, :] = quad[:G, :G] - quad[G:, G:]
-    xa[G : 2 * G, :] = quad[:G, G:] + quad[G:, :G]
-
-    row_of = x_of_row(lax.broadcasted_iota(jnp.int32, (32, G), 1))
-    pick = (row_of == x_pick).astype(f32).astype(bf16)
+        lines_y.append(jnp.concatenate(rows, axis=0))
+
+    patch_y = dot3(split2(jnp.concatenate(lines_y, axis=0)), ty_pair)
+    p_re, p_im = spectrum(at_x, (patch_y[:32], patch_y[32:]))
+    p_re, p_im = xa[0:G, :] + p_re, xa[G : 2 * G, :] + p_im
+    xa[0:G, :] = p_re
+    xa[G : 2 * G, :] = p_im
+
+    from_re, from_im = dot3(to_x_rows, split2(p_re)), dot3(to_x_rows, split2(p_im))
+    t_re, t_im = from_re[:32] - from_im[32:], from_im[:32] + from_re[32:]
+    back = dot3(split2(jnp.concatenate([t_re, t_im], axis=0)), ty_pair)
+    on_patch = back[:32, :G] - back[32:, G:], back[:32, G:] + back[32:, :G]
     line = lax.broadcasted_iota(jnp.int32, (32, G), 1)
     valid = line % 32 // 4 == order % 16 // 8
     rows = []
     for i in range(2):
-        hi, lo = split2(xa[pl.ds(i * G, G), :])
-        here = jnp.where(valid, dot(pick, hi) + dot(pick, lo), 0.0)
+        here = jnp.where(valid, on_patch[i], 0.0)
         rows += [here[0:16], here[16:32]]
     hi, lo = split2(jnp.concatenate(rows, axis=1))
     packed = dot(hi, selc[...]) + dot(lo, selc[...])
@@ -461,6 +475,14 @@
         s3[i] = packed[i : i + 1, :]
     clus_group(lambda to: s3.at[to], x3, p1_s, p1_r)
 
+    back = dot3(split2(xa[...]), ty_pair)
+    local(x3, x3, p1_r).wait()
+    col_group(lambda to: x3, r3, p2_s, p2_r)
+    big[0:G, 0:G] = back[:G, :G] - back[G:, G:]
+    big[0:G, G : 2 * G] = back[:G, G:] + back[G:, :G]
+    quad = dot3(wi, split2(big[0:G, :]))
+    xa[0:G, :] = quad[:G, :G] - quad[G:, G:]
+    xa[G : 2 * G, :] = quad[:G, G:] + quad[G:, :G]
     for kk in range(2):
         tiles = []
         at_cols = pl.ds(kk * 128, 128)
@@ -477,9 +499,6 @@
                     tile = jnp.where(lane == p4, pltpu.roll(tiles[p4], (p4 - k4) % 4 * 32, 2), tile)
             s2[:, kk * 4 + k4] = tile
     clus_group(lambda to: s2.at[to], x2, b1_s, b1_r)
-    local(x3, x3, p1_r).wait()
-    col_group(lambda to: x3, r3, p2_s, p2_r)
-
     collects = h == side
 
     def to_owner(j):
@@ -556,7 +575,7 @@
 
     @pl.when(far)
     def _():
-        lax.fori_loop(5, 16, lambda pair, carry: leave(2 * pair + h, carry), 0)
+        lax.fori_loop(SHARE[0], 16, lambda pair, carry: leave(2 * pair + h, carry), 0)
 
     for l in range(8):
 
@@ -658,7 +677,7 @@
             D((5,)),
             D((3, MOST)),
             D((NCH,)),
-            D((64,)),
+            D((128,)),
             D((NCH,)),
             D((8,)),
             D((8,)),

time: 105 us -> 101 us (0.962)
  Pallas kernels: 104 us -> 100 us
    pallas_call x1, Pallas kernels: 101 us -> 97.3 us  [main_call(): pl.pallas_call(kernel, out_shape=(jax.ShapeDtypeStruct((16, 32, G), f32),...]
where the time goes in v3:
time: 101 us
  Pallas kernels  100 us (99%)
    pallas_call x1, Pallas kernels, main_call(): pl.pallas_call(kernel, out_shape=(jax.ShapeDtypeStruct((16, 32, G), f32),...  97.3 us
    pallas_call x1, Pallas kernels, final_copy(): pl.pallas_call(hand_over, out_shape=tuple((jax.ShapeDtypeStruct(a.shape,...  2.71 us

profile of v3, /device:TPU:1, one launch (start us, length us, event | category | flops | bytes accessed | tf_op | source)
XLA Modules:
  0.0 100.8 jit_solution(13421273766567503249)
XLA Ops:
  0.6 97.3 %shard_map.139 = (f32[16,32,256]{2,1,0:T(8,128)}, bf16[512,1024]{1,0:T(8,128)(2,1)}, bf16[256,512]{1,0:T(8,128)(2,1)}) custom-call(s32[2,4]{1,0:T(2,128)} %pat_ref.1, f32[3]{0:T(128)} %len_ref.1, s32[1,4]{1,0:T(1,128)} %bitcast.1, s32[1,2]{1,0:T(1,128)} %keep_ref.1, bf16[1024,256]{1,0:T(8,128)(2,1)} %margin_ref.1, s32[32]{0:T(128)} %own_ref.1, ...), custom_call_target="tpu_custom_call" | custom-call | flops 12000000000 | bytes 25165824 | tf_op jit(solution)/shard_map/pallas_call | solution.py:629
  97.9 2.7 %shard_map.140 = (f32[16,32,256]{2,1,0:T(8,128)}, bf16[512,1024]{1,0:T(8,128)(2,1)}, bf16[256,512]{1,0:T(8,128)(2,1)}) custom-call(f32[16,32,256]{2,1,0:T(8,128)} %get-tuple-element.6.refs_0_, bf16[512,1024]{1,0:T(8,128)(2,1)} %get-tuple-element.7.refs_1_, bf16[256,512]{1,0:T(8,128)(2,1)} %get-tuple-element.8.refs_2_), custom_call_target="tpu_custom_call" | custom-call | bytes 4194304 | tf_op jit(solution)/shard_map/pallas_call | solution.py:611

commit v4 on v3

--- a/solution.py
+++ b/solution.py
@@ -595,13 +595,18 @@
 
 def hand_over(*refs):
     arrays, outs, held, sem = refs[:3], refs[3:6], refs[6:9], refs[9]
-    into = [pltpu.make_async_copy(arrays[i], held[i], sem.at[i]) for i in range(3)]
-    away = [pltpu.make_async_copy(held[i], outs[i], sem.at[3 + i]) for i in range(3)]
+    into, away = [], []
+    for piece in range(4):
+        for i in range(3):
+            rows = arrays[i].shape[0] // 4
+            at_rows, index = pl.ds(piece * rows, rows), piece * 3 + i
+            into.append(pltpu.make_async_copy(arrays[i].at[at_rows], held[i].at[at_rows], sem.at[index]))
+            away.append(pltpu.make_async_copy(held[i].at[at_rows], outs[i].at[at_rows], sem.at[12 + index]))
     for copy in into:
         copy.start()
-    for i in (2, 0, 1):
-        into[i].wait()
-        away[i].start()
+    for arrived, copy in zip(into, away):
+        arrived.wait()
+        copy.start()
     for copy in away:
         copy.wait()
 
@@ -613,7 +618,7 @@
         out_shape=tuple(jax.ShapeDtypeStruct(a.shape, a.dtype) for a in arrays),
         in_specs=[hbm] * 3,
         out_specs=(hbm,) * 3,
-        scratch_shapes=[pltpu.VMEM(a.shape, a.dtype) for a in arrays] + [pltpu.SemaphoreType.DMA((6,))],
+        scratch_shapes=[pltpu.VMEM(a.shape, a.dtype) for a in arrays] + [pltpu.SemaphoreType.DMA((24,))],
         compiler_params=pltpu.CompilerParams(vmem_limit_bytes=62 << 20),
         cost_estimate=pl.CostEstimate(flops=0, bytes_accessed=4 << 20, transcendentals=0),
     )(*arrays)

time: 101 us -> 101 us (level)
  no operation moved by 1% of the time
where the time goes in v4:
time: 101 us
  Pallas kernels  99.7 us (99%)
    pallas_call x1, Pallas kernels, main_call(): pl.pallas_call(kernel, out_shape=(jax.ShapeDtypeStruct((16, 32, G), f32),...  97.3 us
    pallas_call x1, Pallas kernels, final_copy(): pl.pallas_call(hand_over, out_shape=tuple((jax.ShapeDtypeStruct(a.shape,...  2.42 us

profile of v4, /device:TPU:1, one launch (start us, length us, event | category | flops | bytes accessed | tf_op | source)
XLA Modules:
  0.0 100.5 jit_solution(5469672817564903559)
XLA Ops:
  0.6 97.3 %shard_map.139 = (f32[16,32,256]{2,1,0:T(8,128)}, bf16[512,1024]{1,0:T(8,128)(2,1)}, bf16[256,512]{1,0:T(8,128)(2,1)}) custom-call(s32[2,4]{1,0:T(2,128)} %pat_ref.1, f32[3]{0:T(128)} %len_ref.1, s32[1,4]{1,0:T(1,128)} %bitcast.1, s32[1,2]{1,0:T(1,128)} %keep_ref.1, bf16[1024,256]{1,0:T(8,128)(2,1)} %margin_ref.1, s32[32]{0:T(128)} %own_ref.1, ...), custom_call_target="tpu_custom_call" | custom-call | flops 12000000000 | bytes 25165824 | tf_op jit(solution)/shard_map/pallas_call | solution.py:634
  97.9 2.4 %shard_map.140 = (f32[16,32,256]{2,1,0:T(8,128)}, bf16[512,1024]{1,0:T(8,128)(2,1)}, bf16[256,512]{1,0:T(8,128)(2,1)}) custom-call(f32[16,32,256]{2,1,0:T(8,128)} %get-tuple-element.6.refs_0_, bf16[512,1024]{1,0:T(8,128)(2,1)} %get-tuple-element.7.refs_1_, bf16[256,512]{1,0:T(8,128)(2,1)} %get-tuple-element.8.refs_2_), custom_call_target="tpu_custom_call" | custom-call | bytes 4194304 | tf_op jit(solution)/shard_map/pallas_call | solution.py:616
